TPU v7x, 128 devices: a whole 4x4x4 slice. The times are simulated.
128 devices in a mesh: role: 2 (over z_hi), head: 4 (over z_lo, core), ctx: 16 (over y, x).
Axes of the slice: x: 4, y: 4, z: 4 (z_hi: 2, z_lo: 2; z = z_hi * 2 + z_lo), core: 2. Of those that a mesh axis runs over, the one named last changes fastest.
Arguments:
- history: bfloat16 [2, 2, 4096, 2048], P('role', None, 'ctx'), may hold values from -6 to 6
- queries: bfloat16 [2, 2, 1024, 2048], P('role', None, None, 'head'), may hold values from -150 to 150
- w_kv: bfloat16 [2048, 2, 16, 128], P(None, None, None, 'head'), may hold values from -0.125 to 0.125
- gain: float32 [2048], replicated, may hold values from 0.1 to 1.9
- w_out: bfloat16 [2048, 2048], P('head'), may hold values from -0.5 to 0.5
Outputs:
- attended: bfloat16 [2, 2, 1024, 2048], P('role', None, 'ctx', 'head')
All inputs are finite; a program needn't handle non-finite values.
Results may differ from a plain program's by a relative error of at most 0.02.
The roundings to bfloat16 on the way count: a program that leaves them out, or rounds other values in their place, can miss the bound.
Values may be sent and summed in bfloat16 or wider, within the bound.
A program may use at most 256 MiB of HBM per device.

v0:
```python
import math

import jax
import jax.numpy as jnp
from jax import lax
from jax.sharding import PartitionSpec as P

HD = 128
SEGS_HALF = 2


def partner(block, axis, apart):
    count = lax.axis_size(axis)
    route = []
    for low in range(count):
        high = low | 1 << apart
        if high != low and high < count:
            route += [(low, high), (high, low)]
    return lax.ppermute(block, axis, route)


def merged(value, axis, join):
    pieces = jax.tree.map(lambda part: lax.all_gather(part, axis), value)
    head = jax.tree.map(lambda part: part[0], pieces)
    tail = jax.tree.map(lambda part: part[1:], pieces)
    subtotal, _ = lax.scan(lambda subtotal, slab: (join(subtotal, slab), None), head, tail)
    return subtotal


def merge_parts(left_part, right_part):
    peak_left, total_left, accum_left = left_part
    peak_right, total_right, accum_right = right_part
    global_peak = jnp.maximum(peak_left, peak_right)
    scale_left = jnp.exp(peak_left - global_peak)
    scale_right = jnp.exp(peak_right - global_peak)
    merged_total = total_left * scale_left + total_right * scale_right
    merged_accum = accum_left * scale_left[..., None] + accum_right * scale_right[..., None]
    return (global_peak, merged_total, merged_accum)


def local(history, queries, w_kv, gain, w_out):
    ctx_count = lax.axis_size("ctx")
    heads_local = w_out.shape[0] // HD
    query_count = queries.shape[2]
    rows_own = query_count // ctx_count
    span_rows = min(512, query_count)
    score_scale = 1.0 / math.sqrt(HD)
    outputs = []
    for segment in range(SEGS_HALF):
        row_data = history[0, segment]
        mean_sq = jnp.mean(jnp.square(row_data.astype(jnp.float32)), axis=-1, keepdims=True)
        normed = (row_data.astype(jnp.float32) * lax.rsqrt(mean_sq + 1e-05) * gain).astype(
            jnp.bfloat16
        )
        sliced = jnp.einsum(
            "td,dkne->knet", normed, w_kv, preferred_element_type=jnp.float32
        ).astype(jnp.bfloat16)
        packed = lax.all_to_all(sliced, "head", split_axis=1, concat_axis=2, tiled=True)
        remote = partner(packed, "role", 0)
        key_rows = remote[0]
        value_rows = remote[1]
        query_all = queries[0, segment].reshape(query_count, heads_local, HD)
        peak_list = []
        total_list = []
        accum_list = []
        for offset in range(0, query_count, span_rows):
            query_block = query_all[offset : offset + span_rows]
            scores = (
                jnp.einsum(
                    "qne,net->nqt", query_block, key_rows, preferred_element_type=jnp.float32
                )
                * score_scale
            )
            row_peak = jnp.max(scores, axis=-1)
            probability = jnp.exp(scores - row_peak[..., None]).astype(jnp.bfloat16)
            total_list.append(jnp.sum(probability, axis=-1, dtype=jnp.float32))
            accum_list.append(
                jnp.einsum(
                    "nqt,net->nqe", probability, value_rows, preferred_element_type=jnp.float32
                )
            )
            peak_list.append(row_peak)
        row_peak = jnp.concatenate(peak_list, axis=1)
        row_total = jnp.concatenate(total_list, axis=1)
        row_accum = jnp.concatenate(accum_list, axis=1)
        global_peak, total_all, accum_all = merged(
            (row_peak, row_total, row_accum), "ctx", merge_parts
        )
        row_start = lax.axis_index("ctx") * rows_own
        accum_own = lax.dynamic_slice_in_dim(accum_all, row_start, rows_own, 1)
        total_own = lax.dynamic_slice_in_dim(total_all, row_start, rows_own, 1)
        heads_out = (
            (accum_own / total_own[..., None])
            .transpose(1, 0, 2)
            .reshape(rows_own, heads_local * HD)
            .astype(jnp.bfloat16)
        )
        partial_value = jnp.dot(heads_out, w_out, preferred_element_type=jnp.float32)
        outputs.append(
            lax.psum_scatter(
                partial_value.astype(jnp.bfloat16), "head", scatter_dimension=1, tiled=True
            )
        )
    return jnp.stack(outputs)[None]


def solution(mesh):
    placed = (
        P("role", None, "ctx", None),
        P("role", None, None, "head"),
        P(None, None, None, "head"),
        P(),
        P("head", None),
    )
    return jax.shard_map(
        local, mesh=mesh, in_specs=placed, out_specs=P("role", None, "ctx", "head"), check_vma=False
    )
```

profile of v0, /device:TPU:1, one launch (start us, length us, event | category | flops | bytes accessed | tf_op | source)
XLA Modules:
  0.0 561.5 jit_solution(17860214172831056140)
XLA Ops:
  6.5 2.2 fusion.6
  8.9 3.6 fusion.20
  12.6 12.3 %all_to_all.36 = bf16[2,16,32,256]{3,2,0,1:T(8,128)(2,1)S(1)} all-to-all(bf16[2,16,32,256]{3,2,0,1:T(8,128)(2,1)S(1)} %copy.73), channel_id=1, replica_groups=mesh['role'=2,'head'=4,'ctx'=16] {'head'}, dimensions={1} | all-to-all | bytes 1048576 | tf_op jit(solution)/shard_map/all_to_all | solution.py:58
  26.0 3.3 collective-permute-start.1
  29.3 2.7 fusion.56
  33.4 7.4 %collective-permute-done.1 = bf16[2,4,128,256]{2,3,1,0:T(8,128)(2,1)} collective-permute-done((bf16[2,4,128,256]{2,3,1,0:T(8,128)(2,1)}, bf16[2,4,128,256]{2,3,1,0:T(8,128)(2,1)}, u32[]{:S(2)}, u32[]{:S(2)}) %collective-permute-start.1) | collective-permute-done | bytes 524320 | tf_op jit(solution)/shard_map/ppermute | solution.py:19
  42.2 1.5 bitcast_reduce_fusion.1
  43.8 1.7 fusion.38
  45.5 1.5 fusion.39
  47.0 1.5 pad_maximum_fusion.1
  48.6 3.9 fusion.22
  52.6 11.8 %all_to_all.37 = bf16[2,16,32,256]{3,2,0,1:T(8,128)(2,1)S(1)} all-to-all(bf16[2,16,32,256]{3,2,0,1:T(8,128)(2,1)S(1)} %copy.60), channel_id=1, replica_groups=mesh['role'=2,'head'=4,'ctx'=16] {'head'}, dimensions={1} | all-to-all | bytes 1048576 | tf_op jit(solution)/shard_map/all_to_all | solution.py:58
  65.5 3.0 collective-permute-start
  70.9 8.7 %collective-permute-done = bf16[2,4,128,256]{2,3,1,0:T(8,128)(2,1)} collective-permute-done((bf16[2,4,128,256]{2,3,1,0:T(8,128)(2,1)}, bf16[2,4,128,256]{2,3,1,0:T(8,128)(2,1)}, u32[]{:S(2)}, u32[]{:S(2)}) %collective-permute-start) | collective-permute-done | bytes 524320 | tf_op jit(solution)/shard_map/ppermute | solution.py:19
  81.1 1.6 bitcast_reduce_fusion.3
  82.6 1.7 fusion.34
  84.4 1.6 fusion.35
  87.5 20.1 %all-gather.8 = f32[16,4,1024]{2,1,0:T(4,128)S(1)} all-gather(f32[1,4,1024]{2,1,0:T(4,128)S(1)} %maximum_bitcast_fusion.3), channel_id=5, replica_groups=mesh['role'=2,'head'=4,'ctx'=16] {'ctx'}, dimensions={0}, use_global_device_ids=true | all-gather | bytes 278528 | tf_op jit(solution)/shard_map/all_gather | solution.py:23
  107.6 2.1 convert_reduce_fusion
  110.1 20.6 %all-gather.9 = f32[16,4,1024]{2,1,0:T(4,128)S(1)} all-gather(f32[1,4,1024]{2,1,0:T(4,128)S(1)} %maximum_bitcast_fusion.4), channel_id=6, replica_groups=mesh['role'=2,'head'=4,'ctx'=16] {'ctx'}, dimensions={0}, use_global_device_ids=true | all-gather | bytes 278528 | tf_op jit(solution)/shard_map/all_gather | solution.py:23
  130.6 19.1 %all-gather.6 = f32[16,4,1024]{2,1,0:T(4,128)S(1)} all-gather(f32[1,4,1024]{2,1,0:T(4,128)S(1)} %maximum_bitcast_fusion.1), channel_id=2, replica_groups=mesh['role'=2,'head'=4,'ctx'=16] {'ctx'}, dimensions={0}, use_global_device_ids=true | all-gather | bytes 278528 | tf_op jit(solution)/shard_map/all_gather | solution.py:23
  150.5 20.3 %all-gather.7 = f32[16,4,1024]{2,1,0:T(4,128)S(1)} all-gather(f32[1,4,1024]{2,1,0:T(4,128)S(1)} %maximum_bitcast_fusion.2), channel_id=3, replica_groups=mesh['role'=2,'head'=4,'ctx'=16] {'ctx'}, dimensions={0}, use_global_device_ids=true | all-gather | bytes 278528 | tf_op jit(solution)/shard_map/all_gather | solution.py:23
  170.9 81.4 %all-gather.15.cloned.1.call-done = f32[64,1024,128]{2,1,0:T(8,128)} async-done(((f32[4,1024,128]{2,1,0:T(8,128)}), f32[64,1024,128]{2,1,0:T(8,128)}) %all-gather.15.cloned.1.call-update) | async-done | bytes 33554448 | tf_op jit(solution)/shard_map/all_gather | solution.py:23
  252.3 3.0 slice.142
  255.4 22.7 %slice.145 = f32[60,1024,128]{2,1,0:T(8,128)} slice(f32[64,1024,128]{2,1,0:T(8,128)} %all-gather.15.cloned.1.call-done), slice={[4:64], [0:1024], [0:128]} | slice | bytes 62914560 | tf_op jit(solution)/shard_map/slice | solution.py:25
  278.0 59.0 %while.29 = (s32[]{:T(128)}, f32[4,1024]{1,0:T(4,128)S(1)}, f32[4,1024]{1,0:T(4,128)S(1)}, f32[4,1024,128]{2,1,0:T(8,128)}, f32[15,4,1024]{2,1,0:T(4,128)S(1)}, ...) while((s32[]{:T(128)}, f32[4,1024]{1,0:T(4,128)S(1)}, ...), condition=%wide.region_14.15_spmd, body=%wide.region_13.14_spmd.sunk | while | flops 1597442 | bytes 6455397 | solution.py:26
  278.1 3.8 fusion.76
  282.0 3.9 fusion.76
  285.9 3.8 fusion.76
  289.7 3.9 fusion.76
  293.7 3.8 fusion.76
  297.5 3.8 fusion.76
  301.3 3.8 fusion.76
  305.2 3.8 fusion.76
  309.0 3.8 fusion.76
  312.8 5.0 fusion.76
  317.8 3.8 fusion.76
  321.7 3.8 fusion.76
  325.5 3.8 fusion.76
  329.3 3.9 fusion.76
  333.3 3.8 fusion.76
  337.1 2.1 convolution_convert_fusion
  339.3 111.9 %all-gather.13.cloned.1.call-done = f32[64,1024,128]{2,1,0:T(8,128)} async-done(((f32[4,1024,128]{2,1,0:T(8,128)}), f32[64,1024,128]{2,1,0:T(8,128)}) %all-gather.13.cloned.1.call-update) | async-done | bytes 33554448 | tf_op jit(solution)/shard_map/all_gather | solution.py:23
  451.2 3.0 slice.134
  454.3 22.0 %slice.137 = f32[60,1024,128]{2,1,0:T(8,128)} slice(f32[64,1024,128]{2,1,0:T(8,128)} %all-gather.13.cloned.1.call-done), slice={[4:64], [0:1024], [0:128]} | slice | bytes 62914560 | tf_op jit(solution)/shard_map/slice | solution.py:25
  476.3 57.1 %while.28 = (s32[]{:T(128)}, f32[4,1024]{1,0:T(4,128)S(1)}, f32[4,1024]{1,0:T(4,128)S(1)}, f32[4,1024,128]{2,1,0:T(8,128)}, f32[15,4,1024]{2,1,0:T(4,128)S(1)}, ...) while((s32[]{:T(128)}, f32[4,1024]{1,0:T(4,128)S(1)}, f32[4,1024]{1,0:T(4,128)S(1)}, ...), condition=%wide.region_6.7_spmd, body=%wide.region_5.6_spmd.sunk | while | flops 1597442 | bytes 6455397 | solution.py:26
  476.3 3.8 fusion.74
  480.1 3.8 fusion.74
  483.9 3.8 fusion.74
  487.7 3.8 fusion.74
  491.5 3.8 fusion.74
  495.4 3.8 fusion.74
  499.2 3.8 fusion.74
  503.0 3.8 fusion.74
  506.8 3.8 fusion.74
  510.6 3.8 fusion.74
  514.4 3.8 fusion.74
  518.2 3.8 fusion.74
  522.0 3.8 fusion.74
  525.8 3.8 fusion.74
  529.6 3.8 fusion.74
  533.5 2.1 convolution_convert_fusion.1
  535.7 17.7 %reduce-scatter.3.cloned.1.call-done = bf16[64,512]{1,0:T(8,128)(2,1)} async-done(((bf16[64,2048]{1,0:T(8,128)(2,1)}), bf16[64,512]{1,0:T(8,128)(2,1)}) %reduce-scatter.3.cloned.1.call-update) | async-done | bytes 65552 | tf_op jit(solution)/shard_map/reduce_scatter | solution.py:100
  553.4 1.5 maximum_bitcast_fusion
  (104 shorter events, 13.3 us)
Async XLA Ops:
  6.5 330.6 %copy-start = (bf16[512,2048]{1,0:T(8,128)(2,1)S(1)}, bf16[512,2048]{1,0:T(8,128)(2,1)}, u32[]{:S(2)}) copy-start(bf16[512,2048]{1,0:T(8,128)(2,1)} %param.13) | copy-start | bytes 6291460
  6.5 2.2 copy-start.13
  6.5 245.8 %all-gather.15.cloned.1.call-start = ((), (), s32[]{:S(2)}) async-start(), calls=%async_computation.7 | async-start | bytes 35651584 | tf_op jit(solution)/shard_map/all_gather | solution.py:23
  6.5 2.4 copy-start.8
  26.0 14.8 %collective-permute-start.1 = (bf16[2,4,128,256]{2,3,1,0:T(8,128)(2,1)}, bf16[2,4,128,256]{2,3,1,0:T(8,128)(2,1)}, u32[]{:S(2)}, u32[]{:S(2)}) collective-permute-start(bf16[2,4,128,256]{2,3,1,0:T(8,128)(2,1)} %copy.76), channel_id=1, source_target_pairs={{0,64},{64,0},{1,65},{65,1},{2,66},{66,2},{3,67},{67,3},{4,68},{68... | collective-permute-start | bytes 1572872 | tf_op jit(solution)/shard_map/ppermute | solution.py:19
  42.2 3.3 copy-start.1
  43.7 3.3 copy-start.2
  48.5 402.7 %all-gather.13.cloned.1.call-start = ((), (), s32[]{:S(2)}) async-start(), calls=%async_computation.6 | async-start | bytes 35651584 | tf_op jit(solution)/shard_map/all_gather | solution.py:23
  65.5 14.2 %collective-permute-start = (bf16[2,4,128,256]{2,3,1,0:T(8,128)(2,1)}, bf16[2,4,128,256]{2,3,1,0:T(8,128)(2,1)}, u32[]{:S(2)}, u32[]{:S(2)}) collective-permute-start(bf16[2,4,128,256]{2,3,1,0:T(8,128)(2,1)} %copy.63), channel_id=1, source_target_pairs={{0,64},{64,0},{1,65},{65,1},{2,66},{66,2},{3,67},{67,3},{4,68},{68... | collective-permute-start | bytes 1572872 | tf_op jit(solution)/shard_map/ppermute | solution.py:19
  81.1 3.3 copy-start.4
  82.6 3.3 copy-start.6
  87.4 448.2 %reduce-scatter.5.cloned.1.call-start = ((), (), s32[]{:S(2)}) async-start(), calls=%async_computation.5 | async-start | bytes 327680 | tf_op jit(solution)/shard_map/reduce_scatter | solution.py:100
  87.5 22.2 %copy-start.3 = (f32[4,256,512]{2,1,0:T(8,128)S(1)}, f32[4,256,512]{2,1,0:T(8,128)}, u32[]{:S(2)}) copy-start(f32[4,256,512]{2,1,0:T(8,128)} %copy-done.2) | copy-start | bytes 6291460
  107.6 63.3 %copy-start.9 = (f32[16,4,1024]{2,1,0:T(4,128)}, f32[16,4,1024]{2,1,0:T(4,128)S(1)}, u32[]{:S(2)}) copy-start(f32[16,4,1024]{2,1,0:T(4,128)S(1)} %all-gather.8) | copy-start | bytes 786436
  109.7 40.1 %copy-start.5 = (f32[4,256,512]{2,1,0:T(8,128)S(1)}, f32[4,256,512]{2,1,0:T(8,128)}, u32[]{:S(2)}) copy-start(f32[4,256,512]{2,1,0:T(8,128)} %copy-done.4) | copy-start | bytes 6291460
  110.0 40.1 %copy-start.7 = (f32[4,256,512]{2,1,0:T(8,128)S(1)}, f32[4,256,512]{2,1,0:T(8,128)}, u32[]{:S(2)}) copy-start(f32[4,256,512]{2,1,0:T(8,128)} %copy-done.6) | copy-start | bytes 6291460
  130.6 40.3 %copy-start.10 = (f32[16,4,1024]{2,1,0:T(4,128)}, f32[16,4,1024]{2,1,0:T(4,128)S(1)}, u32[]{:S(2)}) copy-start(f32[16,4,1024]{2,1,0:T(4,128)S(1)} %all-gather.9) | copy-start | bytes 786436
  149.8 21.2 %copy-start.11 = (f32[16,4,1024]{2,1,0:T(4,128)}, f32[16,4,1024]{2,1,0:T(4,128)S(1)}, u32[]{:S(2)}) copy-start(f32[16,4,1024]{2,1,0:T(4,128)S(1)} %all-gather.6) | copy-start | bytes 786436
  170.9 84.5 %copy-start.12 = (f32[16,4,1024]{2,1,0:T(4,128)}, f32[16,4,1024]{2,1,0:T(4,128)S(1)}, u32[]{:S(2)}) copy-start(f32[16,4,1024]{2,1,0:T(4,128)S(1)} %all-gather.7) | copy-start | bytes 786436
  255.4 22.7 %slice-start = ((f32[16,4,1024]{2,1,0:T(4,128)}), f32[15,4,1024]{2,1,0:T(4,128)S(1)}, s32[]{:S(2)}) async-start(f32[16,4,1024]{2,1,0:T(4,128)} %copy-done.9), calls=%async_computation.8 | async-start | bytes 491520 | tf_op jit(solution)/shard_map/slice | solution.py:25
  255.4 22.7 %slice-start.1 = ((f32[16,4,1024]{2,1,0:T(4,128)}), f32[15,4,1024]{2,1,0:T(4,128)S(1)}, s32[]{:S(2)}) async-start(f32[16,4,1024]{2,1,0:T(4,128)} %copy-done.10), calls=%async_computation.9 | async-start | bytes 491520 | tf_op jit(solution)/shard_map/slice | solution.py:25
  339.3 214.1 %reduce-scatter.3.cloned.1.call-start = ((), (), s32[]{:S(2)}) async-start(), calls=%async_computation.4 | async-start | bytes 327680 | tf_op jit(solution)/shard_map/reduce_scatter | solution.py:100
  454.2 22.0 %slice-start.2 = ((f32[16,4,1024]{2,1,0:T(4,128)}), f32[15,4,1024]{2,1,0:T(4,128)S(1)}, s32[]{:S(2)}) async-start(f32[16,4,1024]{2,1,0:T(4,128)} %copy-done.11), calls=%async_computation.10 | async-start | bytes 491520 | tf_op jit(solution)/shard_map/slice | solution.py:25
  454.2 22.0 %slice-start.3 = ((f32[16,4,1024]{2,1,0:T(4,128)}), f32[15,4,1024]{2,1,0:T(4,128)S(1)}, s32[]{:S(2)}) async-start(f32[16,4,1024]{2,1,0:T(4,128)} %copy-done.12), calls=%async_computation.11 | async-start | bytes 491520 | tf_op jit(solution)/shard_map/slice | solution.py:25
Sparse Core Ops, SparseCore 0:
  48.6 203.6 all-gather.14
  254.5 196.6 all-gather.12
  453.6 17.5 reduce-scatter.4
  535.8 17.5 reduce-scatter.2
where the time goes:
time: 563 us; the launch traced here: 561 us
  waiting for transfers between devices  227 us (40%)
  other arithmetic  126 us (22%)
  blocking collectives  104 us (18%)
  local copies, waits for them, and re-layouts  60 us (11%)
  matrix products  24.2 us (4%)
  between operations  13.5 us (2%)
  starting transfers between devices  6.39 us (1%)
    all_gather x2, waiting for transfers between devices, merged(): pieces = jax.tree.map(lambda part: lax.all_gather(part, axis), value)  193 us
    add x30, other arithmetic, merge_parts(): accum_left * scale_left[..., None] + accum_right * scale_right[..., None]  115 us
    all_gather x4, blocking collectives, merged(): pieces = jax.tree.map(lambda part: lax.all_gather(part, axis), value)  80.1 us
    slice x10, local copies, waits for them, and re-layouts, merged(): tail = jax.tree.map(lambda part: part[1:], pieces)  44.7 us
    all_to_all x2, blocking collectives, local(): lax.all_to_all(sliced, 'head', split_axis=1, concat_axis=2, tiled=True)  24.1 us
    reduce_scatter x2, waiting for transfers between devices, local(): lax.psum_scatter(partial_value.astype(jnp.bfloat16), 'head', scatter_dime...  17.7 us
    ppermute x2, waiting for transfers between devices, partner(): return lax.ppermute(block, axis, route)  16.1 us
  transfers between devices with their start and end apart: 6, of which 5 were waited for; matrix products, arithmetic and copies ran while one was open for 35% of the time, Pallas kernels for 0%

commit v1 on v0

v1 whole, which is shorter than its diff:
```python
import math

import jax
import jax.numpy as jnp
from jax import lax
from jax.experimental import pallas as pl
from jax.experimental.pallas import tpu as pltpu
from jax.sharding import PartitionSpec as P

MESH = pl.DeviceIdType.MESH
HD = 128
D = 2048
CHUNKS = 4
KEYS = 256
ROWS = 64
SCALE = math.log2(math.e) / math.sqrt(HD)
NT = (((1,), (1,)), ((), ()))


def merge(parts):
    top = parts[0][1]
    for _, peak, _ in parts[1:]:
        top = jnp.maximum(top, peak)
    accum = total = None
    for part, peak, part_total in parts:
        weight = jnp.exp2((peak - top) * SCALE)
        add = part.astype(jnp.float32) * weight
        accum = add if accum is None else accum + add
        add = part_total * weight
        total = add if total is None else total + add
    return accum, top, total


def kernel(
    hist, quer, w_kv, gain, w_out, out,
    x_buf, xn_buf, g_buf, w_buf, q_buf, wo_buf,
    kv_out, kv_in, a_out, a_ml, a_in, a_in_ml, b_out, b_ml, b_in, b_in_ml,
    p_acc, p_out, p_in,
    x_sem, g_sem, w_sem, q_sem, wo_sem,
    kv_ss, kv_rs, a_ss, a_rs, b_ss, b_rs, p_ss, p_rs,
):
    role, head, ctx = lax.axis_index("role"), lax.axis_index("head"), lax.axis_index("ctx")
    core = head % 2
    x, y = ctx % 4, ctx // 4
    first = (1 - core) * x + core * y
    second = (1 - core) * y + core * x

    def ctx_of(f, g):
        return f * (1 + 3 * core) + g * (4 - 3 * core)

    def a_peer(d):
        return role, head, ctx_of((first + d) % 4, second)

    def b_peer(d):
        return role, head, ctx_of(first, (second + d) % 4)

    def h_peer(d):
        return role, (head + d) % 4, ctx

    barrier = pltpu.get_barrier_semaphore()
    peers = [(1 - role, other, ctx) for other in range(4)]
    for d in range(1, 4):
        peers += [a_peer(d), b_peer(d), h_peer(d)]
    for peer in peers:
        pl.semaphore_signal(barrier, inc=1, device_id=peer, device_id_type=MESH)

    g_copy = pltpu.make_async_copy(gain, g_buf, g_sem)
    g_copy.start()
    x_copies = [pltpu.make_async_copy(hist.at[s], x_buf.at[s], x_sem.at[s]) for s in range(2)]
    for copy in x_copies:
        copy.start()
    w_copies = [
        [pltpu.make_async_copy(w_kv.at[k, :, j], w_buf.at[j, :, k], w_sem.at[j, k]) for k in range(2)]
        for j in range(CHUNKS)
    ]
    for pair in w_copies:
        for copy in pair:
            copy.start()
    q_copies = []
    for s in range(2):
        for f in range(4):
            for g in range(4):
                place = g if s == 0 else g ^ 1
                q_copies.append(
                    pltpu.make_async_copy(
                        quer.at[s, ctx_of(f, g)],
                        q_buf.at[s, f, pl.ds(place * ROWS, ROWS)],
                        q_sem.at[s, f, g],
                    )
                )
    for copy in q_copies:
        copy.start()
    wo_copy = pltpu.make_async_copy(w_out, wo_buf, wo_sem)
    wo_copy.start()

    g_copy.wait()
    for s in range(2):
        x_copies[s].wait()

        def norm(i, carry):
            rows = pl.ds(i * 32, 32)
            values = x_buf[s, rows, :].astype(jnp.float32)
            mean_sq = jnp.mean(values * values, axis=-1, keepdims=True)
            normed = values * lax.rsqrt(mean_sq + 1e-05) * g_buf[...]
            xn_buf[pl.ds(s * KEYS + i * 32, 32), :] = normed.astype(jnp.bfloat16)
            return carry

        lax.fori_loop(0, KEYS // 32, norm, 0)

    def kv_copy(j, other, slot):
        return pltpu.make_async_remote_copy(
            src_ref=kv_out.at[j, other],
            dst_ref=kv_in.at[j, :, pl.ds(pl.multiple_of(slot * 32, 32), 32), :],
            send_sem=kv_ss.at[j, other],
            recv_sem=kv_rs.at[j, slot],
            device_id=(1 - role, other, ctx),
            device_id_type=MESH,
        )

    sends = []
    for j in range(CHUNKS):
        for copy in w_copies[j]:
            copy.wait()
        projected = lax.dot_general(
            w_buf[j].reshape(256, D), xn_buf[...], NT, preferred_element_type=jnp.float32
        )
        kv_out[j] = projected.astype(jnp.bfloat16).reshape(4, 2, 32, 2 * KEYS)
        if j == 0:
            pl.semaphore_wait(barrier, len(peers))
        for other in range(4):
            copy = kv_copy(j, other, head)
            copy.start()
            sends.append(copy)

    for copy in q_copies:
        copy.wait()

    low = lax.broadcasted_iota(jnp.int32, (1, HD), 1) < ROWS
    ones = jnp.ones((16, KEYS), jnp.bfloat16)

    def interleave(left, right):
        pieces = []
        for p in range(2):
            lanes = slice(p * HD, (p + 1) * HD)
            pieces += [
                jnp.where(low, left[:, lanes], right[:, lanes]),
                jnp.where(low, right[:, lanes], left[:, lanes]),
            ]
        return jnp.concatenate(pieces, axis=1)

    def a_copies(j, d):
        f = (first + d) % 4
        return [
            pltpu.make_async_remote_copy(
                src_ref=src.at[j, f],
                dst_ref=dst.at[j, d - 1],
                send_sem=a_ss.at[j, d - 1, i],
                recv_sem=a_rs.at[j, d - 1, i],
                device_id=a_peer(d),
                device_id_type=MESH,
            )
            for i, (src, dst) in enumerate(((a_out, a_in), (a_ml, a_in_ml)))
        ]

    def b_copies(j, d):
        g = (second + d) % 4
        return [
            pltpu.make_async_remote_copy(
                src_ref=src.at[j, g],
                dst_ref=dst.at[j, d - 1],
                send_sem=b_ss.at[j, d - 1, i],
                recv_sem=b_rs.at[j, d - 1, i],
                device_id=b_peer(d),
                device_id_type=MESH,
            )
            for i, (src, dst) in enumerate(((b_out, b_in), (b_ml, b_in_ml)))
        ]

    def attend(j):
        for slot in range(4):
            kv_copy(j, slot, slot).wait_recv()
        keys, values = [], []
        for s in range(2):
            lanes = slice(s * KEYS, (s + 1) * KEYS)
            keys.append(kv_in[j, 0, :, lanes].T)
            values.append(jnp.concatenate([kv_in[j, 1, :, lanes], ones], axis=0))
        for d in (2, 1, 3, 0):
            f = (first + d) % 4
            accums, peaks, totals = [], [], []
            for s in range(2):
                block = q_buf[s, f, :, j * HD : (j + 1) * HD]
                scores = lax.dot_general(keys[s], block, NT, preferred_element_type=jnp.float32)
                peak = jnp.max(scores, axis=0, keepdims=True)
                probability = jnp.exp2((scores - peak) * SCALE).astype(jnp.bfloat16)
                accum = jnp.dot(values[s], probability, preferred_element_type=jnp.float32)
                accums.append(accum[:HD])
                totals.append(accum[HD : HD + 1])
                peaks.append(peak)
            a_out[j, f] = interleave(*accums).astype(jnp.bfloat16)
            a_ml[j, f, 0:1] = interleave(*peaks)
            a_ml[j, f, 1:2] = interleave(*totals)
            if d:
                for copy in a_copies(j, d):
                    copy.start()
                    sends.append(copy)

    def merge_first(j):
        parts = [(a_out[j, first], a_ml[j, first, 0:1], a_ml[j, first, 1:2])]
        for d in range(1, 4):
            for copy in a_copies(j, d):
                copy.wait_recv()
            parts.append((a_in[j, d - 1], a_in_ml[j, d - 1, 0:1], a_in_ml[j, d - 1, 1:2]))
        accum, peak, total = merge(parts)
        accum = accum.astype(jnp.bfloat16)
        for g in range(4):
            lanes = slice(g * HD, (g + 1) * HD)
            b_out[j, g] = accum[:, lanes]
            b_ml[j, g, 0:1] = peak[:, lanes]
            b_ml[j, g, 1:2] = total[:, lanes]
        for d in range(1, 4):
            for copy in b_copies(j, d):
                copy.start()
                sends.append(copy)

    def merge_second(j):
        parts = [(b_out[j, second], b_ml[j, second, 0:1], b_ml[j, second, 1:2])]
        for d in range(1, 4):
            for copy in b_copies(j, d):
                copy.wait_recv()
            parts.append((b_in[j, d - 1], b_in_ml[j, d - 1, 0:1], b_in_ml[j, d - 1, 1:2]))
        accum, _, total = merge(parts)
        rows = (accum / total).T.astype(jnp.bfloat16)
        if j == 0:
            wo_copy.wait()
        for other in range(4):
            part = jnp.dot(
                rows,
                wo_buf[j * HD : (j + 1) * HD, other * 512 : (other + 1) * 512],
                preferred_element_type=jnp.float32,
            )
            if j:
                part = part + p_acc[other]
            p_acc[other] = part

    attend(0)
    for j in range(1, CHUNKS):
        attend(j)
        merge_first(j - 1)
        if j >= 2:
            merge_second(j - 2)
    merge_first(CHUNKS - 1)
    merge_second(CHUNKS - 2)
    merge_second(CHUNKS - 1)

    odd = second % 2
    for other in range(4):
        for p in range(2):
            p_out[other, (odd + p) % 2] = p_acc[other, p * ROWS : (p + 1) * ROWS].astype(jnp.bfloat16)
    p_copies = []
    for d in (2, 1, 3):
        copy = pltpu.make_async_remote_copy(
            src_ref=p_out.at[(head + d) % 4],
            dst_ref=p_in.at[d - 1],
            send_sem=p_ss.at[d - 1],
            recv_sem=p_rs.at[d - 1],
            device_id=h_peer(d),
            device_id_type=MESH,
        )
        copy.start()
        p_copies.append(copy)
    for copy in p_copies:
        copy.wait_recv()
    for p in range(2):
        place = (odd + p) % 2
        total = p_acc[head, p * ROWS : (p + 1) * ROWS]
        for d in range(3):
            total = total + p_in[d, place].astype(jnp.float32)
        out[0, place] = total.astype(jnp.bfloat16)
    for copy in sends + p_copies:
        copy.wait_send()


def local(history, queries, w_kv, gain, w_out):
    bf16, f32 = jnp.bfloat16, jnp.float32
    dma = pltpu.SemaphoreType.DMA
    hist = history.reshape(2, KEYS, D)
    quer = queries.reshape(2, 16, ROWS, 4 * HD)
    w_kv = jnp.transpose(w_kv, (1, 2, 3, 0)).reshape(2, 4, CHUNKS, 32, D)
    return pl.pallas_call(
        kernel,
        out_shape=jax.ShapeDtypeStruct((1, 2, ROWS, 512), bf16),
        in_specs=[pl.BlockSpec(memory_space=pl.ANY)] * 5,
        out_specs=pl.BlockSpec(memory_space=pltpu.VMEM),
        scratch_shapes=[
            pltpu.VMEM((2, KEYS, D), bf16),
            pltpu.VMEM((2 * KEYS, D), bf16),
            pltpu.VMEM((1, D), f32),
            pltpu.VMEM((CHUNKS, 4, 2, 32, D), bf16),
            pltpu.VMEM((2, 4, 4 * ROWS, 4 * HD), bf16),
            pltpu.VMEM((4 * HD, D), bf16),
            pltpu.VMEM((CHUNKS, 4, 2, 32, 2 * KEYS), bf16),
            pltpu.VMEM((CHUNKS, 2, HD, 2 * KEYS), bf16),
            pltpu.VMEM((CHUNKS, 4, HD, 512), bf16),
            pltpu.VMEM((CHUNKS, 4, 2, 512), f32),
            pltpu.VMEM((CHUNKS, 3, HD, 512), bf16),
            pltpu.VMEM((CHUNKS, 3, 2, 512), f32),
            pltpu.VMEM((CHUNKS, 4, HD, HD), bf16),
            pltpu.VMEM((CHUNKS, 4, 2, HD), f32),
            pltpu.VMEM((CHUNKS, 3, HD, HD), bf16),
            pltpu.VMEM((CHUNKS, 3, 2, HD), f32),
            pltpu.VMEM((4, 2 * ROWS, 512), f32),
            pltpu.VMEM((4, 2, ROWS, 512), bf16),
            pltpu.VMEM((3, 2, ROWS, 512), bf16),
            dma((2,)),
            dma,
            dma((CHUNKS, 2)),
            dma((2, 4, 4)),
            dma,
            dma((CHUNKS, 4)),
            dma((CHUNKS, 4)),
            dma((CHUNKS, 3, 2)),
            dma((CHUNKS, 3, 2)),
            dma((CHUNKS, 3, 2)),
            dma((CHUNKS, 3, 2)),
            dma((3,)),
            dma((3,)),
        ],
        compiler_params=pltpu.CompilerParams(
            collective_id=0, has_side_effects=True, vmem_limit_bytes=48 * 2**20
        ),
        cost_estimate=pl.CostEstimate(flops=6 * 10**9, bytes_accessed=10 * 2**20, transcendentals=2**21),
    )(hist, quer, w_kv, gain.reshape(1, D), w_out)


def solution(mesh):
    placed = (
        P("role", None, "ctx", None),
        P("role", None, None, "head"),
        P(None, None, None, "head"),
        P(),
        P("head", None),
    )
    return jax.shard_map(
        local, mesh=mesh, in_specs=placed, out_specs=P("role", None, "ctx", "head"), check_vma=False
    )
```

time: 563 us -> 61.9 us (0.11)
  waiting for transfers between devices: 227 us -> 0 us
  other arithmetic: 126 us -> 0 us
  blocking collectives: 104 us -> 0 us
  Pallas kernels: 0 us -> 57.1 us
  local copies, waits for them, and re-layouts: 60 us -> 4.54 us
  matrix products: 24.2 us -> 0 us
  between operations: 13.5 us -> 0.01 us
  starting transfers between devices: 6.39 us -> 0 us
    all_gather x2 -> x0, waiting for transfers between devices: 193 us -> none  [merged(): pieces = jax.tree.map(lambda part: lax.all_gather(part, axis), value)]
    add x60 -> x0, other arithmetic: 116 us -> none  [the longest x30 115 us: merge_parts(): accum_left * scale_left[..., None] + accum_right * scale_right[..., None]]
    all_gather x4 -> x0, blocking collectives: 80.1 us -> none  [merged(): pieces = jax.tree.map(lambda part: lax.all_gather(part, axis), value)]
    pallas_call x0 -> x1, Pallas kernels: none -> 57.1 us  [local(): pl.pallas_call(kernel, out_shape=jax.ShapeDtypeStruct((1, 2, ROWS, 512),...]
    slice x17 -> x0, local copies, waits for them, and re-layouts: 53.5 us -> none  [the longest x10 44.7 us: merged(): tail = jax.tree.map(lambda part: part[1:], pieces)]
    all_to_all x2 -> x0, blocking collectives: 24.1 us -> none  [local(): lax.all_to_all(sliced, 'head', split_axis=1, concat_axis=2, tiled=True)]
    reduce_scatter x2 -> x0, waiting for transfers between devices: 17.7 us -> none  [local(): lax.psum_scatter(partial_value.astype(jnp.bfloat16), 'head', scatter_dime...]
    dot_general x10 -> x0, matrix products: 16.7 us -> none  [the longest x4 6.55 us: local(): jnp.einsum('nqt,net->nqe', probability, value_rows, preferred_element_typ...]
  transfers between devices with their start and end apart: 6 -> 0, of which waited for: 5 -> 0; matrix products, arithmetic and copies ran while one was open for 35% -> 0% of each run, Pallas kernels for 0% -> 0%
where the time goes in v1:
time: 61.9 us; the launch traced here: 61.7 us
  Pallas kernels  57.1 us (92%)
  local copies, waits for them, and re-layouts  4.54 us (7%)
    pallas_call x1, Pallas kernels, local(): pl.pallas_call(kernel, out_shape=jax.ShapeDtypeStruct((1, 2, ROWS, 512),...  57.1 us
    unnamed x7, local copies, waits for them, and re-layouts  4.54 us

profile of v1, /device:TPU:1, one launch (start us, length us, event | category | flops | bytes accessed | tf_op | source)
XLA Modules:
  0.0 61.7 jit_solution(2249652408499546584)
XLA Ops:
  0.0 0.0 copy-start
  0.0 1.6 %copy-done = bf16[1,2,256,2048]{3,2,1,0:T(8,128)(2,1)S(1)} copy-done((bf16[1,2,256,2048]{3,2,1,0:T(8,128)(2,1)S(1)}, bf16[1,2,256,2048]{3,2,1,0:T(8,128)(2,1)}, u32[]{:S(2)}) %copy-start) | copy-done | bytes 2097176
  1.6 0.0 copy-start.1
  1.6 1.6 %copy-done.1 = bf16[1,2,1024,512]{3,2,1,0:T(8,128)(2,1)S(1)} copy-done((bf16[1,2,1024,512]{3,2,1,0:T(8,128)(2,1)S(1)}, bf16[1,2,1024,512]{3,2,1,0:T(8,128)(2,1)}, u32[]{:S(2)}) %copy-start.1) | copy-done | bytes 2097176
  3.2 0.0 copy-start.2
  3.2 0.7 %copy-done.2 = f32[2048]{0:T(1024)S(1)} copy-done((f32[2048]{0:T(1024)S(1)}, f32[2048]{0:T(1024)}, u32[]{:S(2)}) %copy-start.2) | copy-done | bytes 8216
  3.9 57.1 %shard_map.55 = bf16[1,2,64,512]{3,2,1,0:T(8,128)(2,1)S(1)} custom-call(bf16[2,256,2048]{2,1,0:T(8,128)(2,1)S(1)} %bitcast.6, bf16[2,16,64,512]{3,2,1,0:T(8,128)(2,1)S(1)} %bitcast.7, bf16[2,4,4,32,2048]{4,3,2,1,0:T(8,128)(2,1)} %bitcast.9, f32[1,2048]{1,0:T(1,128)S(1)} %bitcast.8, bf16[512,2048]{1,0:T(8,128)(2,1)} %w_out.1), custom_call_target="tpu_custom_call" | custom-call | flops 6000000000 | bytes 10485760 | tf_op jit(solution)/shard_map/pallas_call | solution.py:289
  61.0 0.7 %copy.7 = bf16[1,2,64,512]{3,2,1,0:T(8,128)(2,1)} copy(bf16[1,2,64,512]{3,2,1,0:T(8,128)(2,1)S(1)} %shard_map.55) | data formatting | bytes 262144
Async XLA Ops:
  0.0 1.6 %copy-start = (bf16[1,2,256,2048]{3,2,1,0:T(8,128)(2,1)S(1)}, bf16[1,2,256,2048]{3,2,1,0:T(8,128)(2,1)}, u32[]{:S(2)}) copy-start(bf16[1,2,256,2048]{3,2,1,0:T(8,128)(2,1)} %param.5) | copy-start | bytes 6291460
  1.6 1.6 %copy-start.1 = (bf16[1,2,1024,512]{3,2,1,0:T(8,128)(2,1)S(1)}, bf16[1,2,1024,512]{3,2,1,0:T(8,128)(2,1)}, u32[]{:S(2)}) copy-start(bf16[1,2,1024,512]{3,2,1,0:T(8,128)(2,1)} %param.6) | copy-start | bytes 6291460
  3.2 0.7 %copy-start.2 = (f32[2048]{0:T(1024)S(1)}, f32[2048]{0:T(1024)}, u32[]{:S(2)}) copy-start(f32[2048]{0:T(1024)} %param.8) | copy-start | bytes 24580

commit v2 on v0

v2 whole, which is shorter than its diff:
```python
import math

import jax
import jax.numpy as jnp
from jax import lax
from jax.experimental import pallas as pl
from jax.experimental.pallas import tpu as pltpu
from jax.sharding import PartitionSpec as P

MESH = pl.DeviceIdType.MESH
HD = 128
D = 2048
CHUNKS = 4
KEYS = 256
ORDER = (0, 1)
ROWS = 64
SCALE = math.log2(math.e) / math.sqrt(HD)
NT = (((1,), (1,)), ((), ()))


def merge(parts):
    top = parts[0][1]
    for _, peak, _ in parts[1:]:
        top = jnp.maximum(top, peak)
    accum = total = None
    for part, peak, part_total in parts:
        weight = jnp.exp2((peak - top) * SCALE)
        add = part.astype(jnp.float32) * weight
        accum = add if accum is None else accum + add
        add = part_total * weight
        total = add if total is None else total + add
    return accum, top, total


def kernel(
    hist, quer, w_kv, gain, w_out, out,
    x_buf, xn_buf, g_buf, w_buf, q_buf, wo_buf,
    kv_out, kv_in, a_out, a_ml, a_in, a_in_ml, b_out, b_ml, b_in, b_in_ml,
    t_buf, ho_buf, p_out, p_in0, p_in1,
    x_sem, g_sem, w_sem, q_sem, wo_sem,
    kv_ss, kv_rs, q_ss, q_rs, a_ss, a_rs, b_ss, b_rs, p0_ss, p0_rs, p1_ss, p1_rs,
):
    role, head, ctx = lax.axis_index("role"), lax.axis_index("head"), lax.axis_index("ctx")
    x, y = ctx % 4, ctx // 4
    place = (x, y)

    def peer_of(axis, d):
        return role, head, (4 * y + (x + d) % 4 if axis == 0 else 4 * ((y + d) % 4) + x)

    def h_peer(d):
        return role, (head + d) % 4, ctx

    def block(g):
        return pl.ds(pl.multiple_of(g * ROWS, ROWS), ROWS)

    def slices(slot):
        return pl.ds(pl.multiple_of(slot * 32, 32), 32)

    barrier = pltpu.get_barrier_semaphore()
    peers = [(1 - role, other, ctx) for other in range(4)]
    for d in range(1, 4):
        peers += [peer_of(0, d), peer_of(1, d), h_peer(d)]
    for peer in peers:
        pl.semaphore_signal(barrier, inc=1, device_id=peer, device_id_type=MESH)

    g_copy = pltpu.make_async_copy(gain, g_buf, g_sem)
    x_copies = [pltpu.make_async_copy(hist.at[s], x_buf.at[s], x_sem.at[s]) for s in range(2)]
    w_copies = [
        [pltpu.make_async_copy(w_kv.at[k, :, j], w_buf.at[j, :, k], w_sem.at[j, k]) for k in range(2)]
        for j in range(CHUNKS)
    ]
    quer_copy = pltpu.make_async_copy(quer.at[0], q_buf.at[0], q_sem)
    wo_copy = pltpu.make_async_copy(w_out, wo_buf, wo_sem)
    g_copy.start()
    x_copies[ORDER[0]].start()
    for pair in w_copies:
        for copy in pair:
            copy.start()
    x_copies[ORDER[1]].start()
    quer_copy.start()
    wo_copy.start()

    sends = []

    def send(copies):
        for copy in copies:
            copy.start()
            sends.append(copy)

    def norm(s):
        x_copies[s].wait()

        def rows_of(i, carry):
            rows = pl.ds(i * 64, 64)
            values = x_buf[s, rows, :].astype(jnp.float32)
            mean_sq = jnp.mean(values * values, axis=-1, keepdims=True)
            normed = values * lax.rsqrt(mean_sq + 1e-05) * g_buf[...]
            xn_buf[s, rows, :] = normed.astype(jnp.bfloat16)
            return carry

        lax.fori_loop(0, KEYS // 64, rows_of, 0)

    def kv_copy(s, j, other, slot):
        return pltpu.make_async_remote_copy(
            src_ref=kv_out.at[s, j, other],
            dst_ref=kv_in.at[s, j, :, slices(slot), :],
            send_sem=kv_ss.at[s, j, other],
            recv_sem=kv_rs.at[s, j, slot],
            device_id=(1 - role if s == 0 else role, other, ctx),
            device_id_type=MESH,
        )

    def project(s, chunks):
        for j in chunks:
            if s == ORDER[0]:
                for copy in w_copies[j]:
                    copy.wait()
            projected = lax.dot_general(
                w_buf[j].reshape(256, D), xn_buf[s], NT, preferred_element_type=jnp.float32
            )
            kv_out[s, j] = projected.astype(jnp.bfloat16).reshape(4, 2, 32, KEYS)
            if s == 0:
                send([kv_copy(s, j, (head + d) % 4, head) for d in (2, 3, 0, 1)])
            else:
                send([kv_copy(s, j, (head + d) % 4, head) for d in (2, 3, 1)])
                kv_in[s, j, :, slices(head), :] = kv_out[s, j, head]

    def q_copy(hop, i, src, dst, peer):
        return pltpu.make_async_remote_copy(
            src_ref=src,
            dst_ref=dst,
            send_sem=q_ss.at[hop, i],
            recv_sem=q_rs.at[hop, i],
            device_id=peer,
            device_id_type=MESH,
        )

    def q_hop(hop, half, d, back):
        columns = slice(half * 256, (half + 1) * 256)
        at = [x, y]
        axis = half if hop == 1 else 1 - half
        if back:
            at[axis] = (at[axis] + 4 - d) % 4
        if hop == 1:
            ref = q_buf.at[1, at[1], at[0], :, columns]
        elif half == 0:
            ref = q_buf.at[1, at[1], :, :, columns]
        else:
            ref = q_buf.at[1, :, at[0], :, columns]
        return q_copy(hop, 3 * half + d - 1, ref, ref, peer_of(axis, d))

    hops = [(half, d) for d in (2, 1, 3) for half in range(2)]
    q_first = q_copy(0, 0, quer.at[1, y, x], q_buf.at[1, y, x], (1 - role, head, ctx))
    a, b = ORDER
    pl.semaphore_wait(barrier, len(peers))
    send([q_first])
    g_copy.wait()
    norm(a)
    project(a, (0,))
    q_first.wait_recv()
    send([q_hop(1, half, d, False) for half, d in hops])
    project(a, (1, 2))
    for half, d in hops:
        q_hop(1, half, d, True).wait_recv()
    send([q_hop(2, half, d, False) for half, d in hops])
    project(a, (3,))
    norm(b)
    project(b, range(CHUNKS))

    ones = jnp.ones((16, KEYS), jnp.bfloat16)

    def a_copies(s, j, d):
        f = (place[j % 2] + d) % 4
        return [
            pltpu.make_async_remote_copy(
                src_ref=src.at[s, j, f],
                dst_ref=dst.at[s, j, d - 1],
                send_sem=a_ss.at[s, j, d - 1, i],
                recv_sem=a_rs.at[s, j, d - 1, i],
                device_id=peer_of(j % 2, d),
                device_id_type=MESH,
            )
            for i, (src, dst) in enumerate(((a_out, a_in), (a_ml, a_in_ml)))
        ]

    def b_copies(s, j, d):
        g = (place[1 - j % 2] + d) % 4 // 2
        return [
            pltpu.make_async_remote_copy(
                src_ref=src.at[s, j, g],
                dst_ref=dst.at[s, j, d - 1],
                send_sem=b_ss.at[s, j, d - 1, i],
                recv_sem=b_rs.at[s, j, d - 1, i],
                device_id=peer_of(1 - j % 2, d),
                device_id_type=MESH,
            )
            for i, (src, dst) in enumerate(((b_out, b_in), (b_ml, b_in_ml)))
        ]

    def wait_inputs(s, j):
        if j == 0:
            if s == 0:
                quer_copy.wait()
            else:
                for half, d in hops:
                    q_hop(2, half, d, True).wait_recv()
        for i in (j, j + 1):
            for d in range(4) if s == 0 else range(1, 4):
                slot = (head + d) % 4
                kv_copy(s, i, slot, slot).wait_recv()

    def attend(s, j):
        keys = kv_in[s, j, 0].T
        values = jnp.concatenate([kv_in[s, j, 1], ones], axis=0)
        columns = slice(j * HD, (j + 1) * HD)
        if j % 2:
            query_rows = q_buf[s, :, :, :, columns].reshape(4 * KEYS, HD)
        else:
            query_rows = jnp.concatenate([q_buf[s, :, g, :, columns].reshape(KEYS, HD) for g in range(4)], axis=0)
        scores = lax.dot_general(keys, query_rows, NT, preferred_element_type=jnp.float32)
        peak = jnp.max(scores, axis=0, keepdims=True)
        probability = jnp.exp2((scores - peak) * SCALE).astype(jnp.bfloat16)
        accum = jnp.dot(values, probability, preferred_element_type=jnp.float32)
        for f in range(4):
            lanes = slice(f * KEYS, (f + 1) * KEYS)
            a_out[s, j, f] = accum[:HD, lanes].astype(jnp.bfloat16)
            a_ml[s, j, f, 0:1] = peak[:, lanes]
            a_ml[s, j, f, 1:2] = accum[HD : HD + 1, lanes]

    def merge_first(s, j):
        own = place[j % 2]
        parts = [(a_out[s, j, own], a_ml[s, j, own, 0:1], a_ml[s, j, own, 1:2])]
        for d in range(3):
            parts.append((a_in[s, j, d], a_in_ml[s, j, d, 0:1], a_in_ml[s, j, d, 1:2]))
        accum, peak, total = merge(parts)
        accum = accum.astype(jnp.bfloat16)
        for g in range(2):
            lanes = slice(g * HD, (g + 1) * HD)
            b_out[s, j, g] = accum[:, lanes]
            b_ml[s, j, g, 0:1] = peak[:, lanes]
            b_ml[s, j, g, 1:2] = total[:, lanes]

    def merge_second(s, j):
        own = place[1 - j % 2] // 2
        parts = [(b_out[s, j, own], b_ml[s, j, own, 0:1], b_ml[s, j, own, 1:2])]
        for d in range(3):
            parts.append((b_in[s, j, d], b_in_ml[s, j, d, 0:1], b_in_ml[s, j, d, 1:2]))
        accum, _, total = merge(parts)
        t_buf[s, j] = (accum / total).T
        ho_buf[s, :, j * HD : (j + 1) * HD] = t_buf[s, j, block(place[1 - j % 2] % 2), :].astype(jnp.bfloat16)

    def exchange(copies, s, j):
        for d in (2, 1, 3):
            pairs = [copies(s, i, d) for i in (j, j + 1)]
            send([pair[n] for n in range(2) for pair in pairs])

    def arrive(copies, s, j):
        for i in (j, j + 1):
            for d in range(1, 4):
                for copy in copies(s, i, d):
                    copy.wait_recv()

    def p_copy(s, d, other, slot):
        src, dst, ss, rs = ((p_out.at[0], p_in0, p0_ss, p0_rs), (p_out.at[1], p_in1, p1_ss, p1_rs))[s]
        return pltpu.make_async_remote_copy(
            src_ref=src.at[other],
            dst_ref=dst.at[d],
            send_sem=ss.at[d],
            recv_sem=rs.at[d],
            device_id=(role if s == 0 else 1 - role, other, ctx),
            device_id_type=MESH,
        )

    def finish(s):
        if s == ORDER[0]:
            wo_copy.wait()
        for other in range(4):
            part = jnp.dot(
                ho_buf[s], wo_buf[:, other * 512 : (other + 1) * 512], preferred_element_type=jnp.float32
            )
            p_out[s, other] = part.astype(jnp.bfloat16)
        send([p_copy(s, d, (head + d) % 4, head) for d in ((2, 1, 3) if s == 0 else (2, 3, 0, 1))])

    pairs = [(s, j) for s in ORDER for j in (0, 2)]
    for u in range(6):
        if u < 4:
            s, j = pairs[u]
            wait_inputs(s, j)
            attend(s, j)
            attend(s, j + 1)
            exchange(a_copies, s, j)
        if 1 <= u <= 4:
            s, j = pairs[u - 1]
            arrive(a_copies, s, j)
            merge_first(s, j)
            merge_first(s, j + 1)
            exchange(b_copies, s, j)
        if u >= 2:
            s, j = pairs[u - 2]
            arrive(b_copies, s, j)
            merge_second(s, j)
            merge_second(s, j + 1)
        if u == 3:
            finish(ORDER[0])
    finish(ORDER[1])
    for s in ORDER:
        total = p_out[0, head].astype(jnp.float32) if s == 0 else None
        for d in range(1, 4) if s == 0 else range(4):
            p_copy(s, d, (head + d) % 4, head).wait_recv()
            part = (p_in0 if s == 0 else p_in1)[d].astype(jnp.float32)
            total = part if total is None else total + part
        out[0, s] = total.astype(jnp.bfloat16)
    for copy in sends:
        copy.wait_send()


def local(history, queries, w_kv, gain, w_out):
    bf16, f32 = jnp.bfloat16, jnp.float32
    dma = pltpu.SemaphoreType.DMA
    hist = history.reshape(2, KEYS, D)
    quer = queries.reshape(2, 4, 4, ROWS, 4 * HD)
    w_kv = jnp.transpose(w_kv, (1, 2, 3, 0)).reshape(2, 4, CHUNKS, 32, D)
    return pl.pallas_call(
        kernel,
        out_shape=jax.ShapeDtypeStruct((1, 2, ROWS, 512), bf16),
        in_specs=[pl.BlockSpec(memory_space=pl.ANY)] * 5,
        out_specs=pl.BlockSpec(memory_space=pltpu.VMEM),
        scratch_shapes=[
            pltpu.VMEM((2, KEYS, D), bf16),
            pltpu.VMEM((2, KEYS, D), bf16),
            pltpu.VMEM((1, D), f32),
            pltpu.VMEM((CHUNKS, 4, 2, 32, D), bf16),
            pltpu.VMEM((2, 4, 4, ROWS, 4 * HD), bf16),
            pltpu.VMEM((4 * HD, D), bf16),
            pltpu.VMEM((2, CHUNKS, 4, 2, 32, KEYS), bf16),
            pltpu.VMEM((2, CHUNKS, 2, HD, KEYS), bf16),
            pltpu.VMEM((2, CHUNKS, 4, HD, KEYS), bf16),
            pltpu.VMEM((2, CHUNKS, 4, 2, KEYS), f32),
            pltpu.VMEM((2, CHUNKS, 3, HD, KEYS), bf16),
            pltpu.VMEM((2, CHUNKS, 3, 2, KEYS), f32),
            pltpu.VMEM((2, CHUNKS, 2, HD, HD), bf16),
            pltpu.VMEM((2, CHUNKS, 2, 2, HD), f32),
            pltpu.VMEM((2, CHUNKS, 3, HD, HD), bf16),
            pltpu.VMEM((2, CHUNKS, 3, 2, HD), f32),
            pltpu.VMEM((2, CHUNKS, HD, HD), f32),
            pltpu.VMEM((2, ROWS, 4 * HD), bf16),
            pltpu.VMEM((2, 4, ROWS, 512), bf16),
            pltpu.VMEM((4, ROWS, 512), bf16),
            pltpu.VMEM((4, ROWS, 512), bf16),
            dma((2,)),
            dma,
            dma((CHUNKS, 2)),
            dma,
            dma,
            dma((2, CHUNKS, 4)),
            dma((2, CHUNKS, 4)),
            dma((3, 6)),
            dma((3, 6)),
            dma((2, CHUNKS, 3, 2)),
            dma((2, CHUNKS, 3, 2)),
            dma((2, CHUNKS, 3, 2)),
            dma((2, CHUNKS, 3, 2)),
            dma((4,)),
            dma((4,)),
            dma((4,)),
            dma((4,)),
        ],
        compiler_params=pltpu.CompilerParams(
            collective_id=0, has_side_effects=True, vmem_limit_bytes=60 * 2**20
        ),
        cost_estimate=pl.CostEstimate(flops=6 * 10**9, bytes_accessed=10 * 2**20, transcendentals=2**21),
    )(hist, quer, w_kv, gain.reshape(1, D), w_out)


def solution(mesh):
    placed = (
        P("role", None, "ctx", None),
        P("role", None, None, "head"),
        P(None, None, None, "head"),
        P(),
        P("head", None),
    )
    return jax.shard_map(
        local, mesh=mesh, in_specs=placed, out_specs=P("role", None, "ctx", "head"), check_vma=False
    )
```

time: 563 us -> 55.7 us (0.10)
  waiting for transfers between devices: 227 us -> 0 us
  other arithmetic: 126 us -> 0 us
  blocking collectives: 104 us -> 0 us
  local copies, waits for them, and re-layouts: 60 us -> 1.57 us
  Pallas kernels: 0 us -> 54 us
  matrix products: 24.2 us -> 0 us
  between operations: 13.5 us -> 0.01 us
  starting transfers between devices: 6.39 us -> 0 us
    all_gather x2 -> x0, waiting for transfers between devices: 193 us -> none  [merged(): pieces = jax.tree.map(lambda part: lax.all_gather(part, axis), value)]
    add x60 -> x0, other arithmetic: 116 us -> none  [the longest x30 115 us: merge_parts(): accum_left * scale_left[..., None] + accum_right * scale_right[..., None]]
    all_gather x4 -> x0, blocking collectives: 80.1 us -> none  [merged(): pieces = jax.tree.map(lambda part: lax.all_gather(part, axis), value)]
    pallas_call x0 -> x1, Pallas kernels: none -> 54 us  [local(): pl.pallas_call(kernel, out_shape=jax.ShapeDtypeStruct((1, 2, ROWS, 512),...]
    slice x17 -> x0, local copies, waits for them, and re-layouts: 53.5 us -> none  [the longest x10 44.7 us: merged(): tail = jax.tree.map(lambda part: part[1:], pieces)]
    all_to_all x2 -> x0, blocking collectives: 24.1 us -> none  [local(): lax.all_to_all(sliced, 'head', split_axis=1, concat_axis=2, tiled=True)]
    reduce_scatter x2 -> x0, waiting for transfers between devices: 17.7 us -> none  [local(): lax.psum_scatter(partial_value.astype(jnp.bfloat16), 'head', scatter_dime...]
    dot_general x10 -> x0, matrix products: 16.7 us -> none  [the longest x4 6.55 us: local(): jnp.einsum('nqt,net->nqe', probability, value_rows, preferred_element_typ...]
  transfers between devices with their start and end apart: 6 -> 0, of which waited for: 5 -> 0; matrix products, arithmetic and copies ran while one was open for 35% -> 0% of each run, Pallas kernels for 0% -> 0%
where the time goes in v2:
time: 55.7 us; the launch traced here: 55.6 us
  Pallas kernels  54 us (97%)
  local copies, waits for them, and re-layouts  1.57 us (3%)
    pallas_call x1, Pallas kernels, local(): pl.pallas_call(kernel, out_shape=jax.ShapeDtypeStruct((1, 2, ROWS, 512),...  54 us
    unnamed x1, local copies, waits for them, and re-layouts  1.57 us

profile of v2, /device:TPU:1, one launch (start us, length us, event | category | flops | bytes accessed | tf_op | source)
XLA Modules:
  0.0 55.6 jit_solution(1761150164234411716)
XLA Ops:
  0.0 54.0 %shard_map.55 = bf16[1,2,64,512]{3,2,1,0:T(8,128)(2,1)} custom-call(bf16[2,256,2048]{2,1,0:T(8,128)(2,1)} %bitcast.7, bf16[2,4,4,64,512]{4,3,2,1,0:T(8,128)(2,1)} %bitcast.8, bf16[2,4,4,32,2048]{4,3,2,1,0:T(8,128)(2,1)} %bitcast.6, f32[1,2048]{1,0:T(1,128)} %bitcast.9, bf16[512,2048]{1,0:T(8,128)(2,1)} %w_out.1), custom_call_target="tpu_custom_call" | custom-call | flops 6000000000 | bytes 10485760 | tf_op jit(solution)/shard_map/pallas_call | solution.py:323
  54.0 1.6 %copy.7 = bf16[1,2,64,512]{3,2,1,0:T(8,128)(2,1)} copy(bf16[1,2,64,512]{3,2,1,0:T(8,128)(2,1)} %shard_map.55) | data formatting | bytes 262144

commit v3 on v2

v3 whole, which is shorter than its diff:
```python
import math

import jax
import jax.numpy as jnp
from jax import lax
from jax.experimental import pallas as pl
from jax.experimental.pallas import tpu as pltpu
from jax.sharding import PartitionSpec as P

MESH = pl.DeviceIdType.MESH
HD = 128
D = 2048
CHUNKS = 4
KEYS = 256
AHEAD = 2
ROWS = 64
SCALE = math.log2(math.e) / math.sqrt(HD)
NT = (((1,), (1,)), ((), ()))


def merge(parts):
    top = parts[0][1]
    for _, peak, _ in parts[1:]:
        top = jnp.maximum(top, peak)
    accum = total = None
    for part, peak, part_total in parts:
        weight = jnp.exp2((peak - top) * SCALE)
        add = part.astype(jnp.float32) * weight
        accum = add if accum is None else accum + add
        add = part_total * weight
        total = add if total is None else total + add
    return accum, top, total


def kernel(
    hist, quer, w_kv, gain, w_out, out,
    x_buf, xn_buf, g_buf, w_buf, q_buf, wo_buf,
    kv_out, kv_in, a_out, a_ml, a_in, a_in_ml, b_out, b_ml, b_in, b_in_ml,
    t_buf, ho_buf, p_out, p_in,
    x_sem, g_sem, w_sem, q_sem, wo_sem,
    kv_ss, kv_rs, a_ss, a_rs, b_ss, b_rs, p_ss, p_rs,
):
    role, head, ctx = lax.axis_index("role"), lax.axis_index("head"), lax.axis_index("ctx")
    x, y = ctx % 4, ctx // 4
    core = head % 2

    def peer_of(axis, d):
        return role, head, 4 * ((y + d * axis) % 4) + (x + d * (1 - axis)) % 4

    def axis_of(j):
        return (j + core) % 2

    def along(axis):
        return x * (1 - axis) + y * axis

    def h_peer(d):
        return role, (head + d) % 4, ctx

    def block(g):
        return pl.ds(pl.multiple_of(g * ROWS, ROWS), ROWS)

    def slices(slot):
        return pl.ds(pl.multiple_of(slot * 32, 32), 32)

    barrier = pltpu.get_barrier_semaphore()
    peers = [(1 - role, other, ctx) for other in range(4)]
    for d in range(1, 4):
        peers += [peer_of(0, d), peer_of(1, d), h_peer(d)]
    for peer in peers:
        pl.semaphore_signal(barrier, inc=1, device_id=peer, device_id_type=MESH)

    g_copy = pltpu.make_async_copy(gain, g_buf, g_sem)
    x_copies = [pltpu.make_async_copy(hist.at[s], x_buf.at[s], x_sem.at[s]) for s in range(2)]
    w_copies = [
        [pltpu.make_async_copy(w_kv.at[k, :, j], w_buf.at[j, :, k], w_sem.at[j, k]) for k in range(2)]
        for j in range(CHUNKS)
    ]
    q_copies = [pltpu.make_async_copy(quer.at[s], q_buf.at[s], q_sem.at[s]) for s in range(2)]
    wo_copy = pltpu.make_async_copy(w_out, wo_buf, wo_sem)
    g_copy.start()
    x_copies[0].start()
    for copy in w_copies[0]:
        copy.start()

    sends = []

    def send(copies):
        for copy in copies:
            copy.start()
            sends.append(copy)

    def norm(s):
        def rows_of(i, carry):
            rows = pl.ds(i * 64, 64)
            values = x_buf[s, rows, :].astype(jnp.float32)
            mean_sq = jnp.mean(values * values, axis=-1, keepdims=True)
            normed = values * lax.rsqrt(mean_sq + 1e-05) * g_buf[...]
            xn_buf[s, rows, :] = normed.astype(jnp.bfloat16)
            return carry

        lax.fori_loop(0, KEYS // 64, rows_of, 0)

    def kv_copy(s, j, other, slot):
        return pltpu.make_async_remote_copy(
            src_ref=kv_out.at[s, j, other],
            dst_ref=kv_in.at[s, j, :, slices(slot), :],
            send_sem=kv_ss.at[s, j, other],
            recv_sem=kv_rs.at[s, j, slot],
            device_id=(1 - role, other, ctx),
            device_id_type=MESH,
        )

    def send_kv(s, j):
        send([kv_copy(s, j, (head + d) % 4, head) for d in (2, 3, 0, 1)])

    def project(s, chunks):
        for j in chunks:
            if s == 0:
                for copy in w_copies[j]:
                    copy.wait()
            projected = lax.dot_general(
                w_buf[j].reshape(256, D), xn_buf[s], NT, preferred_element_type=jnp.float32
            )
            kv_out[s, j] = projected.astype(jnp.bfloat16).reshape(4, 2, 32, KEYS)
            if s == 0 and j == 0:
                pl.semaphore_wait(barrier, len(peers))
            if CHUNKS * s + j < AHEAD:
                send_kv(s, j)

    g_copy.wait()
    x_copies[0].wait()
    for pair in w_copies[1:]:
        for copy in pair:
            copy.start()
    x_copies[1].start()
    norm(0)
    project(0, (0,))
    q_copies[0].start()
    project(0, (1, 2, 3))
    x_copies[1].wait()
    q_copies[1].start()
    wo_copy.start()
    norm(1)
    project(1, range(CHUNKS))

    ones = jnp.ones((16, KEYS), jnp.bfloat16)

    def a_copies(s, j, d):
        f = (along(axis_of(j)) + d) % 4
        return [
            pltpu.make_async_remote_copy(
                src_ref=src.at[s, j, f],
                dst_ref=dst.at[s, j, d - 1],
                send_sem=a_ss.at[s, j, d - 1, i],
                recv_sem=a_rs.at[s, j, d - 1, i],
                device_id=peer_of(axis_of(j), d),
                device_id_type=MESH,
            )
            for i, (src, dst) in enumerate(((a_out, a_in), (a_ml, a_in_ml)))
        ]

    def b_copies(s, j, d):
        g = (along(1 - axis_of(j)) + d) % 4 // 2
        return [
            pltpu.make_async_remote_copy(
                src_ref=src.at[s, j, g],
                dst_ref=dst.at[s, j, d - 1],
                send_sem=b_ss.at[s, j, d - 1, i],
                recv_sem=b_rs.at[s, j, d - 1, i],
                device_id=peer_of(1 - axis_of(j), d),
                device_id_type=MESH,
            )
            for i, (src, dst) in enumerate(((b_out, b_in), (b_ml, b_in_ml)))
        ]

    def wait_inputs(s, j):
        if j == 0:
            q_copies[s].wait()
        for slot in range(4):
            kv_copy(s, j, slot, slot).wait_recv()

    def attend(s, j):
        keys = kv_in[s, j, 0].T
        values = jnp.concatenate([kv_in[s, j, 1], ones], axis=0)
        columns = slice(j * HD, (j + 1) * HD)
        axis = axis_of(j)
        query_rows = jnp.concatenate(
            [
                q_buf[s, f * axis + g * (1 - axis), f * (1 - axis) + g * axis, :, columns]
                for f in range(4)
                for g in range(4)
            ],
            axis=0,
        )
        scores = lax.dot_general(keys, query_rows, NT, preferred_element_type=jnp.float32)
        peak = jnp.max(scores, axis=0, keepdims=True)
        probability = jnp.exp2((scores - peak) * SCALE).astype(jnp.bfloat16)
        accum = jnp.dot(values, probability, preferred_element_type=jnp.float32)
        for f in range(4):
            lanes = slice(f * KEYS, (f + 1) * KEYS)
            a_out[s, j, f] = accum[:HD, lanes].astype(jnp.bfloat16)
            a_ml[s, j, f, 0:1] = peak[:, lanes]
            a_ml[s, j, f, 1:2] = accum[HD : HD + 1, lanes]

    def merge_first(s, j):
        own = along(axis_of(j))
        parts = [(a_out[s, j, own], a_ml[s, j, own, 0:1], a_ml[s, j, own, 1:2])]
        for d in range(3):
            parts.append((a_in[s, j, d], a_in_ml[s, j, d, 0:1], a_in_ml[s, j, d, 1:2]))
        accum, peak, total = merge(parts)
        accum = accum.astype(jnp.bfloat16)
        for g in range(2):
            lanes = slice(g * HD, (g + 1) * HD)
            b_out[s, j, g] = accum[:, lanes]
            b_ml[s, j, g, 0:1] = peak[:, lanes]
            b_ml[s, j, g, 1:2] = total[:, lanes]

    def merge_second(s, j):
        own = along(1 - axis_of(j)) // 2
        parts = [(b_out[s, j, own], b_ml[s, j, own, 0:1], b_ml[s, j, own, 1:2])]
        for d in range(3):
            parts.append((b_in[s, j, d], b_in_ml[s, j, d, 0:1], b_in_ml[s, j, d, 1:2]))
        accum, _, total = merge(parts)
        t_buf[s, j] = (accum / total).T
        ho_buf[s, :, j * HD : (j + 1) * HD] = t_buf[s, j, block(along(1 - axis_of(j)) % 2), :].astype(jnp.bfloat16)

    def exchange(copies, s, j):
        for d in (2, 1, 3):
            send(copies(s, j, d))

    def arrive(copies, s, j):
        for d in range(1, 4):
            for copy in copies(s, j, d):
                copy.wait_recv()

    def p_copy(s, d):
        return pltpu.make_async_remote_copy(
            src_ref=p_out.at[s, (head + d) % 4],
            dst_ref=p_in.at[s, d - 1],
            send_sem=p_ss.at[s, d - 1],
            recv_sem=p_rs.at[s, d - 1],
            device_id=h_peer(d),
            device_id_type=MESH,
        )

    def finish(s):
        if s == 0:
            wo_copy.wait()
        for other in range(4):
            part = jnp.dot(
                ho_buf[s], wo_buf[:, other * 512 : (other + 1) * 512], preferred_element_type=jnp.float32
            )
            p_out[s, other] = part.astype(jnp.bfloat16)
        send([p_copy(s, d) for d in (2, 1, 3)])

    units = [(s, j) for s in range(2) for j in range(CHUNKS)]

    def step_first(u):
        arrive(a_copies, *units[u])
        merge_first(*units[u])
        exchange(b_copies, *units[u])

    def step_second(u):
        arrive(b_copies, *units[u])
        merge_second(*units[u])

    for u in range(8):
        wait_inputs(*units[u])
        if u + AHEAD < 8:
            send_kv(*units[u + AHEAD])
        attend(*units[u])
        exchange(a_copies, *units[u])
        if u >= 2:
            step_first(u - 2)
        if u >= 4:
            step_second(u - 4)
    finish(0)
    step_first(6)
    step_second(4)
    step_second(5)
    step_first(7)
    step_second(6)
    step_second(7)
    finish(1)
    for s in range(2):
        total = p_out[s, head].astype(jnp.float32)
        for d in range(1, 4):
            p_copy(s, d).wait_recv()
            total = total + p_in[s, d - 1].astype(jnp.float32)
        out[0, s] = total.astype(jnp.bfloat16)
    for copy in sends:
        copy.wait_send()


def local(history, queries, w_kv, gain, w_out):
    bf16, f32 = jnp.bfloat16, jnp.float32
    dma = pltpu.SemaphoreType.DMA
    hist = history.reshape(2, KEYS, D)
    quer = queries.reshape(2, 4, 4, ROWS, 4 * HD)
    w_kv = jnp.transpose(w_kv, (1, 2, 3, 0)).reshape(2, 4, CHUNKS, 32, D)
    return pl.pallas_call(
        kernel,
        out_shape=jax.ShapeDtypeStruct((1, 2, ROWS, 512), bf16),
        in_specs=[pl.BlockSpec(memory_space=pl.ANY)] * 5,
        out_specs=pl.BlockSpec(memory_space=pltpu.VMEM),
        scratch_shapes=[
            pltpu.VMEM((2, KEYS, D), bf16),
            pltpu.VMEM((2, KEYS, D), bf16),
            pltpu.VMEM((1, D), f32),
            pltpu.VMEM((CHUNKS, 4, 2, 32, D), bf16),
            pltpu.VMEM((2, 4, 4, ROWS, 4 * HD), bf16),
            pltpu.VMEM((4 * HD, D), bf16),
            pltpu.VMEM((2, CHUNKS, 4, 2, 32, KEYS), bf16),
            pltpu.VMEM((2, CHUNKS, 2, HD, KEYS), bf16),
            pltpu.VMEM((2, CHUNKS, 4, HD, KEYS), bf16),
            pltpu.VMEM((2, CHUNKS, 4, 2, KEYS), f32),
            pltpu.VMEM((2, CHUNKS, 3, HD, KEYS), bf16),
            pltpu.VMEM((2, CHUNKS, 3, 2, KEYS), f32),
            pltpu.VMEM((2, CHUNKS, 2, HD, HD), bf16),
            pltpu.VMEM((2, CHUNKS, 2, 2, HD), f32),
            pltpu.VMEM((2, CHUNKS, 3, HD, HD), bf16),
            pltpu.VMEM((2, CHUNKS, 3, 2, HD), f32),
            pltpu.VMEM((2, CHUNKS, HD, HD), f32),
            pltpu.VMEM((2, ROWS, 4 * HD), bf16),
            pltpu.VMEM((2, 4, ROWS, 512), bf16),
            pltpu.VMEM((2, 3, ROWS, 512), bf16),
            dma((2,)),
            dma,
            dma((CHUNKS, 2)),
            dma((2,)),
            dma,
            dma((2, CHUNKS, 4)),
            dma((2, CHUNKS, 4)),
            dma((2, CHUNKS, 3, 2)),
            dma((2, CHUNKS, 3, 2)),
            dma((2, CHUNKS, 3, 2)),
            dma((2, CHUNKS, 3, 2)),
            dma((2, 3)),
            dma((2, 3)),
        ],
        compiler_params=pltpu.CompilerParams(
            collective_id=0, has_side_effects=True, vmem_limit_bytes=60 * 2**20
        ),
        cost_estimate=pl.CostEstimate(flops=6 * 10**9, bytes_accessed=10 * 2**20, transcendentals=2**21),
    )(hist, quer, w_kv, gain.reshape(1, D), w_out)


def solution(mesh):
    placed = (
        P("role", None, "ctx", None),
        P("role", None, None, "head"),
        P(None, None, None, "head"),
        P(),
        P("head", None),
    )
    return jax.shard_map(
        local, mesh=mesh, in_specs=placed, out_specs=P("role", None, "ctx", "head"), check_vma=False
    )
```

time: 55.7 us -> 53.8 us (0.966)
  Pallas kernels: 54 us -> 51.8 us
    pallas_call x1, Pallas kernels: 54 us -> 51.8 us  [local(): pl.pallas_call(kernel, out_shape=jax.ShapeDtypeStruct((1, 2, ROWS, 512),...]
where the time goes in v3:
time: 53.8 us; the launch traced here: 53.4 us
  Pallas kernels  51.8 us (96%)
  local copies, waits for them, and re-layouts  1.57 us (3%)
    pallas_call x1, Pallas kernels, local(): pl.pallas_call(kernel, out_shape=jax.ShapeDtypeStruct((1, 2, ROWS, 512),...  51.8 us
    unnamed x1, local copies, waits for them, and re-layouts  1.57 us

profile of v3, /device:TPU:1, one launch (start us, length us, event | category | flops | bytes accessed | tf_op | source)
XLA Modules:
  0.0 53.4 jit_solution(886454586968501801)
XLA Ops:
  0.0 51.8 %shard_map.55 = bf16[1,2,64,512]{3,2,1,0:T(8,128)(2,1)} custom-call(bf16[2,256,2048]{2,1,0:T(8,128)(2,1)} %bitcast.7, bf16[2,4,4,64,512]{4,3,2,1,0:T(8,128)(2,1)} %bitcast.8, bf16[2,4,4,32,2048]{4,3,2,1,0:T(8,128)(2,1)} %bitcast.6, f32[1,2048]{1,0:T(1,128)} %bitcast.9, bf16[512,2048]{1,0:T(8,128)(2,1)} %w_out.1), custom_call_target="tpu_custom_call" | custom-call | flops 6000000000 | bytes 10485760 | tf_op jit(solution)/shard_map/pallas_call | solution.py:301
  51.8 1.6 %copy.7 = bf16[1,2,64,512]{3,2,1,0:T(8,128)(2,1)} copy(bf16[1,2,64,512]{3,2,1,0:T(8,128)(2,1)} %shard_map.55) | data formatting | bytes 262144

commit v4 on v3

--- a/solution.py
+++ b/solution.py
@@ -111,7 +111,7 @@
         )
 
     def send_kv(s, j):
-        send([kv_copy(s, j, (head + d) % 4, head) for d in (2, 3, 0, 1)])
+        send([kv_copy(s, j, (head + d) % 4, head) for d in (0, 1, 2, 3)])
 
     def project(s, chunks):
         for j in chunks:

time: 53.8 us -> 53.1 us (0.987)
  no operation moved by 1% of the time
where the time goes in v4:
time: 53.1 us; the launch traced here: 52.9 us
  Pallas kernels  51.3 us (97%)
  local copies, waits for them, and re-layouts  1.57 us (3%)
    pallas_call x1, Pallas kernels, local(): pl.pallas_call(kernel, out_shape=jax.ShapeDtypeStruct((1, 2, ROWS, 512),...  51.3 us
    unnamed x1, local copies, waits for them, and re-layouts  1.57 us

profile of v4, /device:TPU:1, one launch (start us, length us, event | category | flops | bytes accessed | tf_op | source)
XLA Modules:
  0.0 52.9 jit_solution(12758622526494711979)
XLA Ops:
  0.0 51.3 %shard_map.55 = bf16[1,2,64,512]{3,2,1,0:T(8,128)(2,1)} custom-call(bf16[2,256,2048]{2,1,0:T(8,128)(2,1)} %bitcast.7, bf16[2,4,4,64,512]{4,3,2,1,0:T(8,128)(2,1)} %bitcast.8, bf16[2,4,4,32,2048]{4,3,2,1,0:T(8,128)(2,1)} %bitcast.6, f32[1,2048]{1,0:T(1,128)} %bitcast.9, bf16[512,2048]{1,0:T(8,128)(2,1)} %w_out.1), custom_call_target="tpu_custom_call" | custom-call | flops 6000000000 | bytes 10485760 | tf_op jit(solution)/shard_map/pallas_call | solution.py:301
  51.3 1.6 %copy.7 = bf16[1,2,64,512]{3,2,1,0:T(8,128)(2,1)} copy(bf16[1,2,64,512]{3,2,1,0:T(8,128)(2,1)} %shard_map.55) | data formatting | bytes 262144
